TPU v7x, 32 devices: a whole 2x2x4 slice. The times are simulated.
32 devices in a mesh: img: 4 (over y, x), band: 8 (over z, core).
Axes of the slice: x: 2, y: 2, z: 4, core: 2. Of those that a mesh axis runs over, the one named last changes fastest.
Arguments:
- latents: bfloat16 [4, 16, 64, 1120], P('img', 'band'), may hold values from -6 to 6
- tangents: bfloat16 [4, 16, 64, 1120], P('img', 'band'), may hold values from -6 to 6
- w_expand: bfloat16 [1120, 5632], P('img', 'band'), may hold values from -0.1875 to 0.1875
- b_expand: bfloat16 [5632], P('band'), may hold values from -3 to 3
- w_depth: bfloat16 [9, 5632], P(None, 'band'), may hold values from -2 to 2
- b_depth: bfloat16 [5632], P('band'), may hold values from -3 to 3
Outputs:
- gated: bfloat16 [4, 16, 64, 2816], P('img', 'band')
- gated_tangent: bfloat16 [4, 16, 64, 2816], P('img', 'band')
All inputs are finite; a program needn't handle non-finite values.
Results may differ from a plain program's by a relative error of at most 0.0057.
Values may be sent and summed in bfloat16 or wider, within the bound.
A program may use at most 64 MiB of HBM per device.

v0:
```python
import jax
import jax.numpy as jnp
from jax import lax
from jax.sharding import PartitionSpec as P


def extended(cells, sides, width):
    for axis, dim in sides:
        count = lax.axis_size(axis)
        ends = count - 1
        head = lax.slice_in_dim(cells, 0, width, axis=dim)
        tail = lax.slice_in_dim(cells, cells.shape[dim] - width, cells.shape[dim], axis=dim)
        cells = jnp.concatenate(
            [
                lax.ppermute(tail, axis, [(i, (i + 1) % count) for i in range(ends)]),
                cells,
                lax.ppermute(head, axis, [((i + 1) % count, i) for i in range(ends)]),
            ],
            axis=dim,
        )
    return cells


def tangent_act(primal_pre, tangent_pre):
    sigmoid_v = jax.nn.sigmoid(primal_pre)
    value = primal_pre * sigmoid_v
    slope = sigmoid_v * (1.0 + primal_pre * (1.0 - sigmoid_v))
    return (value, slope * tangent_pre)


def depthwise(padded, depth_taps, row_count, col_count):
    total = jnp.zeros(padded.shape[:-3] + (row_count, col_count, padded.shape[-1]), jnp.float32)
    for row_off in range(3):
        for col_off in range(3):
            window = padded[
                ..., row_off : row_off + row_count, col_off : col_off + col_count, :
            ].astype(jnp.float32)
            total = total + window * depth_taps[3 * row_off + col_off].astype(jnp.float32)
    return total


def finish(mixed, depth_bias, half):
    primal_mix = mixed[0] + depth_bias.astype(jnp.float32)
    tangent_mix = mixed[1]
    gate_value, gate_tangent = tangent_act(primal_mix[..., half:], tangent_mix[..., half:])
    gated = primal_mix[..., :half] * gate_value
    gated_tangent = tangent_mix[..., :half] * gate_value + primal_mix[..., :half] * gate_tangent
    return (gated.astype(jnp.bfloat16), gated_tangent.astype(jnp.bfloat16))


def activate(pre_act, expand_bias, token_count):
    bias_cols = expand_bias.astype(jnp.float32)
    value, slope_tangent = tangent_act(pre_act[:token_count] + bias_cols, pre_act[token_count:])
    return jnp.concatenate([value.astype(jnp.bfloat16), slope_tangent.astype(jnp.bfloat16)], 0)


def on_device(latents, tangents, w_expand, b_expand, w_depth, b_depth):
    image_count, row_count, col_count, channels = latents.shape
    depth_taps, expand_bias, depth_bias = (
        lax.all_gather(w_depth, "band", axis=1, tiled=True),
        lax.all_gather(b_expand, "band", axis=0, tiled=True),
        lax.all_gather(b_depth, "band", axis=0, tiled=True),
    )
    full_width = expand_bias.shape[0]
    half = full_width // 2
    both_inputs = jnp.stack([latents, tangents])
    both_inputs = extended(both_inputs, (("band", 2),), 1)
    span_rows = both_inputs.shape[2]
    token_count = image_count * span_rows * col_count
    stacked = both_inputs.reshape(2 * token_count, channels)
    weight_rows = lax.all_gather(w_expand, "img", axis=0, tiled=True)
    pre_act = jnp.dot(
        stacked,
        lax.all_gather(weight_rows, "band", axis=1, tiled=True),
        preferred_element_type=jnp.float32,
    )
    activated = activate(pre_act, expand_bias, token_count)
    activated = activated.reshape(2, image_count, span_rows, col_count, full_width)
    band_count = lax.axis_size("band")
    global_row = lax.axis_index("band") * row_count + jnp.arange(span_rows, dtype=jnp.int32) - 1
    inside = (global_row >= 0) & (global_row < band_count * row_count)
    padded = jnp.where(inside[None, None, :, None, None], activated, jnp.zeros_like(activated))
    padded = jnp.pad(padded, ((0, 0), (0, 0), (0, 0), (1, 1), (0, 0)))
    mixed = depthwise(padded, depth_taps, row_count, col_count)
    return finish(mixed, depth_bias, half)


def solution(mesh):
    placed = (
        P("img", "band", None, None),
        P("img", "band", None, None),
        P("img", "band"),
        P("band"),
        P(None, "band"),
        P("band"),
    )
    return jax.shard_map(
        on_device,
        mesh=mesh,
        in_specs=placed,
        out_specs=(P("img", "band", None, None), P("img", "band", None, None)),
        check_vma=False,
    )
```

profile of v0, /device:TPU:0, one launch (start us, length us, event | category | flops | bytes accessed | tf_op | source)
XLA Modules:
  0.0 206.6 jit_solution(1353635090246530111)
XLA Ops:
  7.2 0.0 copy-start.5
  7.2 0.0 copy-start
  7.2 0.0 copy-start.1
  7.2 0.0 copy-start.3
  7.2 0.0 copy-start.4
  7.2 0.0 copy-start.2
  7.2 0.0 all-gather.4.cloned.1.call-start
  7.3 0.7 all-gather.4.cloned.1.call-update
  8.0 0.0 all-gather.6.cloned.1.call-start
  8.0 36.8 %all-gather.4.cloned.1.call-done = bf16[1120,704]{1,0:T(8,128)(2,1)} async-done(((bf16[280,704]{1,0:T(8,128)(2,1)}), bf16[1120,704]{1,0:T(8,128)(2,1)}) %all-gather.4.cloned.1.call-update) | async-done | bytes 1576976 | tf_op jit(solution)/shard_map/all_gather | solution.py:71
  44.8 3.8 %copy.14 = bf16[1120,704]{0,1:T(8,128)(2,1)} copy(bf16[1120,704]{1,0:T(8,128)(2,1)} %all-gather.4.cloned.1.call-done) | data formatting | bytes 3153920 | tf_op jit(solution)/shard_map/all_gather | solution.py:71
  48.6 0.0 all-gather.6.cloned.1.call-update
  48.6 1.2 fusion.6
  49.8 1.8 collective-permute-start
  51.6 1.3 collective-permute-start.1
  52.9 0.0 copy-done.5
  52.9 0.6 dynamic-slice
  54.2 0.0 copy-done.3
  54.2 0.2 dynamic-update-slice
  54.4 0.0 copy-done.4
  54.4 0.2 dynamic-update-slice.1
  54.7 0.0 copy-done.2
  54.7 20.6 %all-gather = bf16[8,704,9]{1,2,0:T(8,128)(2,1)S(1)} all-gather(bf16[1,704,9]{1,2,0:T(8,128)(2,1)S(1)} %bitcast.28), channel_id=1, replica_groups=mesh['img'=4,'band'=8] {'band'}, dimensions={0}, use_global_device_ids=true | all-gather | bytes 114048 | tf_op jit(solution)/shard_map/all_gather | solution.py:60
  75.3 32.5 %all-reduce.3 = (bf16[5632]{0:T(1024)(128)(2,1)S(1)}, bf16[5632]{0:T(1024)(128)(2,1)S(1)}) all-reduce(bf16[5632]{0:T(1024)(128)(2,1)S(1)} %dynamic-update-slice, bf16[5632]{0:T(1024)(128)(2,1)S(1)} %dynamic-update-slice.1), channel_id=1, replica_groups=mesh['img'=4,'band'=8] {'band'}, use_global_device_ids=true, to_apply=%add.1 | all-reduce | flops 11264 | bytes 45056
  107.8 0.2 reshape.147
  108.0 0.6 fusion.15
  108.6 0.0 collective-permute-done
  108.6 0.0 collective-permute-done.1
  108.6 0.0 copy-done
  108.6 0.0 copy-done.1
  108.6 0.2 pad_maximum_fusion.1
  108.8 62.2 %all-gather.6.cloned.1.call-done = bf16[1120,5632]{0,1:T(8,128)(2,1)} async-done(((bf16[1120,704]{0,1:T(8,128)(2,1)}), bf16[1120,5632]{0,1:T(8,128)(2,1)}) %all-gather.6.cloned.1.call-update) | async-done | bytes 12615696 | tf_op jit(solution)/shard_map/all_gather | solution.py:74
  171.0 13.2 %fusion.16 = f32[512,5632]{1,0:T(8,128)} fusion(bf16[512,1120]{1,0:T(8,128)(2,1)S(1)} %bitcast.26, bf16[1120,5632]{0,1:T(8,128)(2,1)} %all-gather.6.cloned.1.call-done), kind=kOutput, calls=%fused_computation.49 | convolution fusion | flops 6459228160 | bytes 25296896 | tf_op jit(solution)/shard_map/dot_general | solution.py:72
  184.2 5.6 %multiply_convert_fusion = (bf16[256,5632]{1,0:T(8,128)(2,1)S(1)}, bf16[256,5632]{1,0:T(8,128)(2,1)S(1)}) fusion(f32[512,5632]{1,0:T(8,128)} %fusion.16, f32[5632]{0:T(1024)S(1)} %convert_element_type.137), kind=kLoop, calls=%fused_computation.5 | loop fusion | flops 17301504 | bytes 17324032 | tf_op jit(solution)/shard_map/convert_element_type | solution.py:54
  189.8 0.4 pad_maximum_fusion
  190.2 0.4 broadcast_select_fusion
  190.6 6.8 %multiply_add_fusion = f32[2,1,2,64,5632]{4,3,2,1,0:T(8,128)S(1)} fusion(bf16[2,1,4,64,5632]{4,3,2,1,0:T(8,128)(2,1)S(1)} %broadcast_select_fusion, f32[5632]{0:T(1024)S(1)} %get-tuple-element.3, f32[5632]{0:T(1024)S(1)} %get-tuple-element.4, f32[5632]{0:T(1024)S(1)} %get-tuple-element.5, f32[5632]{0:T(1024)S(1)} %get-tuple-element.6, ...), kind=kLoop, calls=%fused_computation.4 | loop fusion | flops 37486592 | bytes 20406272 | tf_op jit(solution)/shard_map/add | solution.py:38
  197.4 0.2 slice_bitcast_fusion
  197.6 0.3 fusion.1
  197.9 1.9 fusion.4
  (6 shorter events, 0.1 us)
Async XLA Ops:
  7.2 45.8 %copy-start.5 = (u32[32]{0:T(128)S(1)}, u32[32]{0:T(128)}, u32[]{:S(2)}) copy-start(u32[32]{0:T(128)} %constant.26) | copy-start | bytes 388
  7.2 101.4 %copy-start = (bf16[1,2,64,1120]{3,2,1,0:T(8,128)(2,1)S(1)}, bf16[1,2,64,1120]{3,2,1,0:T(8,128)(2,1)}, u32[]{:S(2)}) copy-start(bf16[1,2,64,1120]{3,2,1,0:T(8,128)(2,1)} %param.6) | copy-start | bytes 860164
  7.2 101.4 %copy-start.1 = (bf16[1,2,64,1120]{3,2,1,0:T(8,128)(2,1)S(1)}, bf16[1,2,64,1120]{3,2,1,0:T(8,128)(2,1)}, u32[]{:S(2)}) copy-start(bf16[1,2,64,1120]{3,2,1,0:T(8,128)(2,1)} %param.7) | copy-start | bytes 860164
  7.2 47.0 %copy-start.3 = (bf16[704]{0:T(1024)(128)(2,1)S(1)}, bf16[704]{0:T(1024)(128)(2,1)}, u32[]{:S(2)}) copy-start(bf16[704]{0:T(1024)(128)(2,1)} %param.9) | copy-start | bytes 4228
  7.2 47.2 %copy-start.4 = (bf16[704]{0:T(1024)(128)(2,1)S(1)}, bf16[704]{0:T(1024)(128)(2,1)}, u32[]{:S(2)}) copy-start(bf16[704]{0:T(1024)(128)(2,1)} %param.11) | copy-start | bytes 4228
  7.2 47.5 %copy-start.2 = (bf16[9,704]{1,0:T(8,128)(2,1)S(1)}, bf16[9,704]{1,0:T(8,128)(2,1)}, u32[]{:S(2)}) copy-start(bf16[9,704]{1,0:T(8,128)(2,1)} %param.10) | copy-start | bytes 38020
  7.2 37.6 %all-gather.4.cloned.1.call-start = ((), (), s32[]{:S(2)}) async-start(), calls=%async_computation | async-start | bytes 2150400 | tf_op jit(solution)/shard_map/all_gather | solution.py:71
  8.0 163.1 %all-gather.6.cloned.1.call-start = ((), (), s32[]{:S(2)}) async-start(), calls=%async_computation.1 | async-start | bytes 14598144 | tf_op jit(solution)/shard_map/all_gather | solution.py:74
  49.8 58.7 %collective-permute-start = (bf16[2,1,1,64,1120]{4,3,2,1,0:T(8,128)(2,1)S(1)}, bf16[2,1,1,64,1120]{4,3,2,1,0:T(8,128)(2,1)S(1)}, u32[]{:S(2)}, u32[]{:S(2)}) collective-permute-start(bf16[2,1,1,64,1120]{4,3,2,1,0:T(8,128)(2,1)S(1)} %get-tuple-element.17), channel_id=1, source_target_pairs={{0,1},{1,2},{2,3},{3,4},{4,5},{5,6},{6,7},{8,9},{9,10},{10,11},{11... | collective-permute-start | bytes 860168 | tf_op jit(solution)/shard_map/ppermute | solution.py:15
  51.6 57.0 %collective-permute-start.1 = (bf16[2,1,1,64,1120]{4,3,2,1,0:T(8,128)(2,1)S(1)}, bf16[2,1,1,64,1120]{4,3,2,1,0:T(8,128)(2,1)S(1)}, u32[]{:S(2)}, u32[]{:S(2)}) collective-permute-start(bf16[2,1,1,64,1120]{4,3,2,1,0:T(8,128)(2,1)S(1)} %get-tuple-element.18), channel_id=1, source_target_pairs={{1,0},{2,1},{3,2},{4,3},{5,4},{6,5},{7,6},{9,8},{10,9},{11,10},{12... | collective-permute-start | bytes 860168 | tf_op jit(solution)/shard_map/ppermute | solution.py:17
Sparse Core Ops, SparseCore 0:
  9.9 34.8 all-gather.3
  48.8 122.2 all-gather.5
where the time goes:
time: 207 us
  waiting for transfers between devices  99.8 us (48%)
  blocking collectives  53.1 us (26%)
  other arithmetic  17.3 us (8%)
  between operations  14.9 us (7%)
  matrix products  13.2 us (6%)
  local copies, waits for them, and re-layouts  5.28 us (3%)
  starting transfers between devices  3.12 us (2%)
    all_gather x1, waiting for transfers between devices, on_device(): lax.all_gather(weight_rows, 'band', axis=1, tiled=True)  62.2 us
    all_gather x1, waiting for transfers between devices, on_device(): weight_rows = lax.all_gather(w_expand, 'img', axis=0, tiled=True)  36.8 us
    unnamed x1, blocking collectives  32.5 us
    all_gather x1, blocking collectives, on_device(): lax.all_gather(w_depth, 'band', axis=1, tiled=True)  20.6 us
    dot_general x1, matrix products, on_device(): jnp.dot(stacked, lax.all_gather(weight_rows, 'band', axis=1, tiled=True),...  13.2 us
    add x1, other arithmetic, depthwise(): total + window * depth_taps[3 * row_off + col_off].astype(jnp.float32)  6.79 us
    convert_element_type x1, other arithmetic, activate(): value.astype(jnp.bfloat16)  5.6 us
  transfers between devices with their start and end apart: 4, of which 2 were waited for; matrix products, arithmetic and copies ran while one was open for 2% of the time, Pallas kernels for 0%

commit v1 on v0

--- a/solution.py
+++ b/solution.py
@@ -1,6 +1,8 @@
 import jax
 import jax.numpy as jnp
 from jax import lax
+from jax.experimental import pallas as pl
+from jax.experimental.pallas import tpu as pltpu
 from jax.sharding import PartitionSpec as P
 
 
@@ -85,6 +87,375 @@
     return finish(mixed, depth_bias, half)
 
 
+MESH = pl.DeviceIdType.MESH
+PIECE = 256
+
+
+def round_up(size, unit):
+    return -(-size // unit) * unit
+
+
+def act_slope(v):
+    sig = jax.nn.sigmoid(v)
+    return v * sig, sig * (1.0 + v * (1.0 - sig))
+
+
+def fused_kernel(
+    acts_ref, w_ref, par_ref, out_ref,
+    abuf, wbuf, pbuf, ebuf, stage,
+    acts_sem, halo_send, halo_recv, par_send, par_recv, w_send, w_recv, out_send, out_recv,
+):
+    depth = 4
+    pieces = w_ref.shape[0]
+    rows = acts_ref.shape[1]
+    cols = acts_ref.shape[2]
+    span = 2 * rows + 2
+    img = lax.axis_index("img")
+    band = lax.axis_index("band")
+    z = band // 2
+    core = band % 2
+    sib = z * 2 + (1 - core)
+    px, py = img % 2, img // 2
+    img_x = py * 2 + (1 - px)
+    img_y = (1 - py) * 2 + px
+    img_d = (1 - py) * 2 + (1 - px)
+
+    barrier = pltpu.get_barrier_semaphore()
+    for other in range(1, 2 * depth):
+        pl.semaphore_signal(
+            barrier, inc=1, device_id=(img, lax.rem(band + other, 2 * depth)), device_id_type=MESH
+        )
+    for other in (img_x, img_y):
+        pl.semaphore_signal(barrier, inc=1, device_id=(other, band), device_id_type=MESH)
+    pl.semaphore_wait(barrier, 2 * depth + 1)
+
+    def remote(src, dst, send, recv, device):
+        return pltpu.make_async_remote_copy(
+            src_ref=src, dst_ref=dst, send_sem=send, recv_sem=recv, device_id=device, device_id_type=MESH
+        )
+
+    first = 1 + rows * core
+    keep = pltpu.make_async_copy(acts_ref, abuf.at[:, pl.ds(first, rows)], acts_sem.at[0])
+    keep.start()
+    share = remote(acts_ref, abuf.at[:, pl.ds(first, rows)], acts_sem.at[1], acts_sem.at[2], (img, sib))
+    share.start()
+
+    def halo_up(to):
+        return remote(
+            acts_ref.at[:, rows - 1], abuf.at[:, 0], halo_send.at[to], halo_recv.at[0],
+            (img, 2 * (z + 1) + to),
+        )
+
+    def halo_down(to):
+        return remote(
+            acts_ref.at[:, 0], abuf.at[:, span - 1], halo_send.at[to], halo_recv.at[1],
+            (img, 2 * (z - 1) + to),
+        )
+
+    sends_up = (core == 1) & (z < depth - 1)
+    sends_down = (core == 0) & (z > 0)
+
+    @pl.when(sends_up)
+    def _():
+        halo_up(0).start()
+        halo_up(1).start()
+
+    @pl.when(sends_down)
+    def _():
+        halo_down(0).start()
+        halo_down(1).start()
+
+    def par_copy(step):
+        to = lax.rem(z + step, depth)
+        return remote(par_ref, pbuf.at[z], par_send.at[step], par_recv.at[z], (img, 2 * to + core))
+
+    for step in range(1, depth):
+        par_copy(step).start()
+    pbuf[z] = par_ref[...]
+
+    def w_copy(route, src, zz, p, column):
+        device = (
+            (img_x, band), (img_y, band), (img, band + 2), (img, band - 2)
+        )[route]
+        return remote(
+            src, wbuf.at[zz, p, column], w_send.at[route, zz, p, column], w_recv.at[zz, p, column], device
+        )
+
+    def arrived(zz, p, column):
+        w_copy(0, wbuf.at[zz, p, column], zz, p, column).wait_recv()
+
+    def own_sends(p):
+        src = w_ref.at[p]
+
+        @pl.when(z < depth - 1)
+        def _():
+            w_copy(2, src, z, p, img).start()
+
+        @pl.when(z > 0)
+        def _():
+            w_copy(3, src, z, p, img).start()
+
+        w_copy(0, src, z, p, img).start()
+        w_copy(1, src, z, p, img).start()
+
+    def forward_z(p):
+        for dist in range(1, depth):
+            @pl.when(z - dist >= 0)
+            def _():
+                zz = z - dist
+                arrived(zz, p, img)
+
+                @pl.when(z < depth - 1)
+                def _():
+                    w_copy(2, wbuf.at[zz, p, img], zz, p, img).start()
+
+                w_copy(0, wbuf.at[zz, p, img], zz, p, img).start()
+                w_copy(1, wbuf.at[zz, p, img], zz, p, img).start()
+
+            @pl.when(z + dist < depth)
+            def _():
+                zz = z + dist
+                arrived(zz, p, img)
+
+                @pl.when(z > 0)
+                def _():
+                    w_copy(3, wbuf.at[zz, p, img], zz, p, img).start()
+
+                w_copy(0, wbuf.at[zz, p, img], zz, p, img).start()
+                w_copy(1, wbuf.at[zz, p, img], zz, p, img).start()
+
+    def forward_xy(p):
+        for dist in range(depth):
+            zz = lax.rem(z + dist, depth)
+            arrived(zz, p, img_x)
+            arrived(zz, p, img_y)
+
+            @pl.when(zz % 2 == 0)
+            def _():
+                w_copy(1, wbuf.at[zz, p, img_x], zz, p, img_x).start()
+
+            @pl.when(zz % 2 == 1)
+            def _():
+                w_copy(0, wbuf.at[zz, p, img_y], zz, p, img_y).start()
+
+    def out_copy(step):
+        p, q = step // 2, step % 2
+        return remote(
+            stage.at[step], out_ref.at[2 * q + core, p], out_send.at[step], out_recv.at[step], (img, sib)
+        )
+
+    row_id = lax.broadcasted_iota(jnp.int32, (cols, 128), 0)
+
+    def compute(step):
+        p, q = step // 2, step % 2
+        for half in range(2):
+            zz = q + (depth // 2) * half
+            weights = wbuf[zz, p].reshape(-1, PIECE)
+
+            def product(t, _):
+                tokens = abuf[t].reshape(span * cols, -1)
+                pre = jnp.dot(tokens, weights, preferred_element_type=jnp.float32)
+                ebuf[half, t] = pre.reshape(span, cols, PIECE)
+                return 0
+
+            lax.fori_loop(0, 2, product, 0)
+            bias = pbuf[zz, p][0:1].astype(jnp.float32)
+
+            def activation(r, _):
+                value, slope = act_slope(ebuf[half, 0, r] + bias)
+                inside = ((z > 0) | (r > 0)) & ((z < depth - 1) | (r < span - 1))
+                scale = jnp.where(inside, 1.0, 0.0)
+                ebuf[half, 0, r] = value * scale
+                ebuf[half, 1, r] = slope * ebuf[half, 1, r] * scale
+                return 0
+
+            lax.fori_loop(0, span, activation, 0)
+
+        par = [pbuf[q, p].astype(jnp.float32), pbuf[q + depth // 2, p].astype(jnp.float32)]
+
+        def mixed(half, t, o, lanes):
+            taps = par[half][:, lanes]
+            cells = [ebuf[half, t, o + k, :, lanes] for k in range(3)]
+            sums = []
+            for c in range(3):
+                total = cells[0] * taps[1 + c : 2 + c]
+                for k in (1, 2):
+                    total = total + cells[k] * taps[1 + 3 * k + c : 2 + 3 * k + c]
+                sums.append(total)
+            before = jnp.where(row_id == 0, 0.0, pltpu.roll(sums[0], 1, 0))
+            after = jnp.where(row_id == cols - 1, 0.0, pltpu.roll(sums[2], cols - 1, 0))
+            return sums[1] + before + after
+
+        def gate(o, store):
+            for lane in range(0, PIECE, 128):
+                lanes = slice(lane, lane + 128)
+                pv = mixed(0, 0, o, lanes) + par[0][10:11, lanes]
+                pg = mixed(1, 0, o, lanes) + par[1][10:11, lanes]
+                tv = mixed(0, 1, o, lanes)
+                tg = mixed(1, 1, o, lanes)
+                value, slope = act_slope(pg)
+                store(lanes, (pv * value).astype(jnp.bfloat16), (tv * value + pv * slope * tg).astype(jnp.bfloat16))
+
+        def theirs(j, _):
+            def store(lanes, a, b):
+                stage[step, 0, j, :, lanes] = a
+                stage[step, 1, j, :, lanes] = b
+
+            gate(rows * (1 - core) + j, store)
+            return 0
+
+        lax.fori_loop(0, rows, theirs, 0)
+        out_copy(step).start()
+
+        def ours(j, _):
+            def store(lanes, a, b):
+                out_ref[2 * q + core, p, 0, j, :, lanes] = a
+                out_ref[2 * q + core, p, 1, j, :, lanes] = b
+
+            gate(rows * core + j, store)
+            return 0
+
+        lax.fori_loop(0, rows, ours, 0)
+
+    for p in range(pieces):
+        own_sends(p)
+
+    def place(p, _):
+        wbuf[z, p, img] = w_ref[p]
+        return 0
+
+    lax.fori_loop(0, pieces, place, 0)
+
+    @pl.when(z == 0)
+    def _():
+        abuf[:, 0] = jnp.zeros(abuf.shape[:1] + abuf.shape[2:], abuf.dtype)
+
+    @pl.when(z == depth - 1)
+    def _():
+        abuf[:, span - 1] = jnp.zeros(abuf.shape[:1] + abuf.shape[2:], abuf.dtype)
+
+    lax.fori_loop(0, 2, lambda p, _: (forward_z(p), 0)[1], 0)
+    forward_xy(0)
+    lax.fori_loop(2, pieces, lambda p, _: (forward_z(p), 0)[1], 0)
+
+    keep.wait()
+    share.wait()
+
+    @pl.when(z > 0)
+    def _():
+        halo_up(0).wait_recv()
+
+    @pl.when(z < depth - 1)
+    def _():
+        halo_down(0).wait_recv()
+
+    for step in range(1, depth):
+        source = lax.rem(z + step, depth)
+        remote(
+            par_ref, pbuf.at[source], par_send.at[step], par_recv.at[source], (img, 2 * source + core)
+        ).wait_recv()
+
+    def turn(step, _):
+        p, q = step // 2, step % 2
+
+        @pl.when((q == 1) & (p + 1 < pieces))
+        def _():
+            forward_xy(p + 1)
+
+        arrived(q, p, img_d)
+        arrived(q + depth // 2, p, img_d)
+        compute(step)
+        return 0
+
+    lax.fori_loop(0, 2 * pieces, turn, 0)
+
+    for step in range(1, depth):
+        par_copy(step).wait_send()
+
+    @pl.when(sends_up)
+    def _():
+        halo_up(0).wait_send()
+        halo_up(1).wait_send()
+
+    @pl.when(sends_down)
+    def _():
+        halo_down(0).wait_send()
+        halo_down(1).wait_send()
+
+    def sent(p, _):
+        for zz in range(depth):
+            w_copy(0, w_ref.at[p], zz, p, img).wait_send()
+            w_copy(1, w_ref.at[p], zz, p, img).wait_send()
+            if zz % 2 == 0:
+                w_copy(1, w_ref.at[p], zz, p, img_x).wait_send()
+            else:
+                w_copy(0, w_ref.at[p], zz, p, img_y).wait_send()
+
+            @pl.when((z >= zz) & (z < depth - 1))
+            def _():
+                w_copy(2, w_ref.at[p], zz, p, img).wait_send()
+
+            @pl.when((z <= zz) & (z > 0))
+            def _():
+                w_copy(3, w_ref.at[p], zz, p, img).wait_send()
+
+        return 0
+
+    lax.fori_loop(0, pieces, sent, 0)
+
+    def returned(step, _):
+        out_copy(step).wait()
+        return 0
+
+    lax.fori_loop(0, 2 * pieces, returned, 0)
+
+
+def fused(latents, tangents, w_expand, b_expand, w_depth, b_depth):
+    _, rows, cols, channels = latents.shape
+    part, width = w_expand.shape
+    parts = channels // part
+    tall = round_up(part, 16)
+    pieces = round_up(width, PIECE) // PIECE
+    wide = pieces * PIECE
+    acts = jnp.stack([latents[0], tangents[0]]).reshape(2, rows, cols, parts, part)
+    acts = jnp.pad(acts, ((0, 0),) * 4 + ((0, tall - part),)).reshape(2, rows, cols, parts * tall)
+    weights = jnp.pad(w_expand, ((0, tall - part), (0, wide - width)))
+    weights = weights.reshape(tall, pieces, PIECE).transpose(1, 0, 2)
+    par = jnp.concatenate([b_expand[None], w_depth, b_depth[None]], 0)
+    par = jnp.pad(par, ((0, 16 - par.shape[0]), (0, wide - width)))
+    par = par.reshape(16, pieces, PIECE).transpose(1, 0, 2)
+    bf, f32 = jnp.bfloat16, jnp.float32
+    dma = pltpu.SemaphoreType.DMA
+    out = pl.pallas_call(
+        fused_kernel,
+        out_shape=jax.ShapeDtypeStruct((4, pieces, 2, rows, cols, PIECE), bf),
+        in_specs=[pl.BlockSpec(memory_space=pltpu.VMEM)] * 3,
+        out_specs=pl.BlockSpec(memory_space=pltpu.VMEM),
+        scratch_shapes=[
+            pltpu.VMEM((2, 2 * rows + 2, cols, parts * tall), bf),
+            pltpu.VMEM((4, pieces, parts, tall, PIECE), bf),
+            pltpu.VMEM((4, pieces, 16, PIECE), bf),
+            pltpu.VMEM((2, 2, 2 * rows + 2, cols, PIECE), f32),
+            pltpu.VMEM((2 * pieces, 2, rows, cols, PIECE), bf),
+            dma((3,)),
+            dma((2,)),
+            dma((2,)),
+            dma((4,)),
+            dma((4,)),
+            dma((4, 4, pieces, parts)),
+            dma((4, pieces, parts)),
+            dma((2 * pieces,)),
+            dma((2 * pieces,)),
+        ],
+        compiler_params=pltpu.CompilerParams(
+            collective_id=0, has_side_effects=True, vmem_limit_bytes=40 * 1024 * 1024
+        ),
+    )(acts, weights, par)
+    out = out.transpose(2, 3, 4, 0, 1, 5).reshape(2, rows, cols, 4, wide)[..., :width]
+    out = out.reshape(2, 1, rows, cols, 4 * width)
+    return out[0], out[1]
+
+
 def solution(mesh):
     placed = (
         P("img", "band", None, None),
@@ -94,8 +465,11 @@
         P(None, "band"),
         P("band"),
     )
+    body = on_device
+    if mesh.shape["img"] == 4 and mesh.shape["band"] == 8:
+        body = fused
     return jax.shard_map(
-        on_device,
+        body,
         mesh=mesh,
         in_specs=placed,
         out_specs=(P("img", "band", None, None), P("img", "band", None, None)),

time: 207 us -> 103 us (0.50)
  waiting for transfers between devices: 99.8 us -> 0 us
  Pallas kernels: 0 us -> 87.4 us
  blocking collectives: 53.1 us -> 0 us
  other arithmetic: 17.3 us -> 0.84 us
  between operations: 14.9 us -> 0.75 us
  matrix products: 13.2 us -> 0 us
  local copies, waits for them, and re-layouts: 5.28 us -> 14 us
  starting transfers between devices: 3.12 us -> 0 us
    all_gather x2 -> x0, waiting for transfers between devices: 99.1 us -> none  [the longest x1 62.2 us: on_device(): lax.all_gather(weight_rows, 'band', axis=1, tiled=True)]
    pallas_call x0 -> x1, Pallas kernels: none -> 87.4 us  [fused(): pl.pallas_call(fused_kernel, out_shape=jax.ShapeDtypeStruct((4, pieces, 2...]
    unnamed x1 -> x0, blocking collectives: 32.5 us -> none
    all_gather x1 -> x0, blocking collectives: 20.6 us -> none  [on_device(): lax.all_gather(w_depth, 'band', axis=1, tiled=True)]
    dot_general x1 -> x0, matrix products: 13.2 us -> none  [on_device(): jnp.dot(stacked, lax.all_gather(weight_rows, 'band', axis=1, tiled=True),...]
    convert_element_type x5 -> x0, other arithmetic: 8.02 us -> none  [the longest x1 5.6 us: activate(): value.astype(jnp.bfloat16)]
    add x2 -> x0, other arithmetic: 7.07 us -> none  [the longest x1 6.79 us: depthwise(): total + window * depth_taps[3 * row_off + col_off].astype(jnp.float32)]
    reshape x0 -> x5, local copies, waits for them, and re-layouts: none -> 4.13 us  [the longest x1 2.9 us: fused(): out.transpose(2, 3, 4, 0, 1, 5).reshape(2, rows, cols, 4, wide)[..., :width]]
  transfers between devices with their start and end apart: 4 -> 0, of which waited for: 2 -> 0; matrix products, arithmetic and copies ran while one was open for 2% -> 0% of each run, Pallas kernels for 0% -> 0%
where the time goes in v1:
time: 103 us
  Pallas kernels  87.4 us (85%)
  local copies, waits for them, and re-layouts  14 us (14%)
    pallas_call x1, Pallas kernels, fused(): pl.pallas_call(fused_kernel, out_shape=jax.ShapeDtypeStruct((4, pieces, 2...  87.4 us
    squeeze x2, local copies, waits for them, and re-layouts, fused(): return (out[0], out[1])  2.98 us
    reshape x1, local copies, waits for them, and re-layouts, fused(): out.transpose(2, 3, 4, 0, 1, 5).reshape(2, rows, cols, 4, wide)[..., :width]  2.9 us
    slice x3, local copies, waits for them, and re-layouts, fused(): return (out[0], out[1])  2.69 us

profile of v1, /device:TPU:0, one launch (start us, length us, event | category | flops | bytes accessed | tf_op | source)
XLA Modules:
  0.0 103.0 jit_solution(6042877391744835695)
XLA Ops:
  0.6 0.0 copy-start
  0.6 0.0 copy-start.1
  0.6 0.7 broadcast_in_dim.6
  1.4 0.7 broadcast_in_dim.7
  2.1 0.8 fusion.8
  2.9 1.1 %pad.13 = bf16[288,768]{1,0:T(8,128)(2,1)S(1)} pad(bf16[280,704]{1,0:T(8,128)(2,1)} %param.8, bf16[]{:T(256)} %constant.2.clone.1), padding=0_8x0_64 | pad | bytes 836610 | tf_op jit(solution)/shard_map/jit(_pad)/pad | solution.py:422
  3.9 0.0 copy-done
  4.0 0.0 copy-done.1
  4.0 0.1 pad_maximum_fusion
  4.0 0.7 reshape.24
  4.8 0.3 pad.12
  5.1 0.5 reshape.25.acts_ref
  5.6 87.4 %shard_map.77 = bf16[4,3,2,2,64,256]{5,4,3,2,1,0:T(8,128)(2,1)S(1)} custom-call(bf16[2,2,64,1152]{3,2,1,0:T(8,128)(2,1)S(1)} %reshape.25.acts_ref, bf16[3,288,256]{2,1,0:T(8,128)(2,1)S(1)} %bitcast.20, bf16[3,16,256]{2,1,0:T(8,128)(2,1)S(1)} %bitcast.21), custom_call_target="tpu_custom_call" | custom-call | tf_op jit(solution)/shard_map/pallas_call | solution.py:429
  93.0 1.4 %copy.13 = bf16[2,2,64,4,3,256]{5,4,2,3,1,0:T(4,128)(2,1)S(1)} copy(bf16[2,2,64,4,3,256]{5,2,1,0,4,3:T(8,128)(2,1)S(1)} %bitcast.19) | data formatting | bytes 3145728 | tf_op jit(solution)/shard_map/transpose | solution.py:454
  94.4 2.9 %reshape.28 = bf16[2,2,64,4,768]{4,2,3,1,0:T(8,128)(2,1)} reshape(bf16[2,2,64,4,3,256]{5,4,2,3,1,0:T(4,128)(2,1)S(1)} %copy.13) | data formatting | bytes 3145728 | tf_op jit(solution)/shard_map/reshape | solution.py:454
  97.3 1.5 %fusion.9 = (bf16[1,2,64,4,704]{4,2,3,1,0:T(8,128)(2,1)S(1)}, bf16[1,2,64,4,704]{4,2,3,1,0:T(8,128)(2,1)S(1)}) fusion(bf16[2,2,64,4,768]{4,2,3,1,0:T(8,128)(2,1)} %reshape.28), kind=kLoop, calls=%fused_computation.14 | loop fusion | bytes 2883584 | tf_op jit(solution)/shard_map/slice | solution.py:456
  98.8 0.6 copy.15
  99.4 1.5 %squeeze.7 = bf16[1,2,64,2816]{3,2,1,0:T(8,128)(2,1)} reshape(bf16[1,2,64,4,704]{4,3,2,1,0:T(4,128)(2,1)S(1)} %copy.15) | data formatting | bytes 1441792 | tf_op jit(solution)/shard_map/squeeze | solution.py:456
  100.9 0.6 copy.14
  101.5 1.5 %squeeze.6 = bf16[1,2,64,2816]{3,2,1,0:T(8,128)(2,1)} reshape(bf16[1,2,64,4,704]{4,3,2,1,0:T(4,128)(2,1)S(1)} %copy.14) | data formatting | bytes 1441792 | tf_op jit(solution)/shard_map/squeeze | solution.py:456
  (2 shorter events, 0.0 us)
Async XLA Ops:
  0.6 3.3 %copy-start = (bf16[1,2,64,1120]{3,2,1,0:T(8,128)(2,1)S(1)}, bf16[1,2,64,1120]{3,2,1,0:T(8,128)(2,1)}, u32[]{:S(2)}) copy-start(bf16[1,2,64,1120]{3,2,1,0:T(8,128)(2,1)} %param.7) | copy-start | bytes 860164
  0.6 3.3 %copy-start.1 = (bf16[1,2,64,1120]{3,2,1,0:T(8,128)(2,1)S(1)}, bf16[1,2,64,1120]{3,2,1,0:T(8,128)(2,1)}, u32[]{:S(2)}) copy-start(bf16[1,2,64,1120]{3,2,1,0:T(8,128)(2,1)} %param.6) | copy-start | bytes 860164

commit v2 on v1

--- a/solution.py
+++ b/solution.py
@@ -101,14 +101,14 @@
 
 
 def fused_kernel(
-    acts_ref, w_ref, par_ref, out_ref,
-    abuf, wbuf, pbuf, ebuf, stage,
+    latents_ref, tangents_ref, w_ref, par_ref, gated_ref, tangent_ref,
+    abuf, wbuf, pbuf, ebuf, stage, out_ref, line,
     acts_sem, halo_send, halo_recv, par_send, par_recv, w_send, w_recv, out_send, out_recv,
 ):
     depth = 4
-    pieces = w_ref.shape[0]
-    rows = acts_ref.shape[1]
-    cols = acts_ref.shape[2]
+    pieces = w_ref.shape[1] // PIECE
+    _, rows, cols, channels = latents_ref.shape
+    parts = wbuf.shape[2]
     span = 2 * rows + 2
     img = lax.axis_index("img")
     band = lax.axis_index("band")
@@ -134,45 +134,6 @@
             src_ref=src, dst_ref=dst, send_sem=send, recv_sem=recv, device_id=device, device_id_type=MESH
         )
 
-    first = 1 + rows * core
-    keep = pltpu.make_async_copy(acts_ref, abuf.at[:, pl.ds(first, rows)], acts_sem.at[0])
-    keep.start()
-    share = remote(acts_ref, abuf.at[:, pl.ds(first, rows)], acts_sem.at[1], acts_sem.at[2], (img, sib))
-    share.start()
-
-    def halo_up(to):
-        return remote(
-            acts_ref.at[:, rows - 1], abuf.at[:, 0], halo_send.at[to], halo_recv.at[0],
-            (img, 2 * (z + 1) + to),
-        )
-
-    def halo_down(to):
-        return remote(
-            acts_ref.at[:, 0], abuf.at[:, span - 1], halo_send.at[to], halo_recv.at[1],
-            (img, 2 * (z - 1) + to),
-        )
-
-    sends_up = (core == 1) & (z < depth - 1)
-    sends_down = (core == 0) & (z > 0)
-
-    @pl.when(sends_up)
-    def _():
-        halo_up(0).start()
-        halo_up(1).start()
-
-    @pl.when(sends_down)
-    def _():
-        halo_down(0).start()
-        halo_down(1).start()
-
-    def par_copy(step):
-        to = lax.rem(z + step, depth)
-        return remote(par_ref, pbuf.at[z], par_send.at[step], par_recv.at[z], (img, 2 * to + core))
-
-    for step in range(1, depth):
-        par_copy(step).start()
-    pbuf[z] = par_ref[...]
-
     def w_copy(route, src, zz, p, column):
         device = (
             (img_x, band), (img_y, band), (img, band + 2), (img, band - 2)
@@ -184,8 +145,11 @@
     def arrived(zz, p, column):
         w_copy(0, wbuf.at[zz, p, column], zz, p, column).wait_recv()
 
+    def piece_of(p):
+        return w_ref.at[:, pl.ds(pl.multiple_of(p * PIECE, PIECE), PIECE)]
+
     def own_sends(p):
-        src = w_ref.at[p]
+        src = piece_of(p)
 
         @pl.when(z < depth - 1)
         def _():
@@ -197,6 +161,59 @@
 
         w_copy(0, src, z, p, img).start()
         w_copy(1, src, z, p, img).start()
+
+    for p in range(pieces):
+        own_sends(p)
+
+    first = 1 + rows * core
+    part = channels // parts
+    tall = w_ref.shape[0]
+    lane_id = lax.broadcasted_iota(jnp.int32, line.shape, 1)
+    line[:, channels:] = jnp.zeros((cols, line.shape[1] - channels), jnp.float32)
+    for t, source_ref in enumerate((latents_ref, tangents_ref)):
+        for r in range(rows):
+            line[:, :channels] = source_ref[0, r].astype(jnp.float32)
+            cells = line[...]
+            spread = cells
+            for i in range(1, parts):
+                spread = jnp.where(lane_id >= tall * i, pltpu.roll(cells, (tall - part) * i, 1), spread)
+            abuf[t, first + r] = spread.astype(jnp.bfloat16)
+    own_rows = abuf.at[:, pl.ds(first, rows)]
+    share = remote(own_rows, own_rows, acts_sem.at[0], acts_sem.at[1], (img, sib))
+    share.start()
+
+    def halo_up(to):
+        return remote(
+            abuf.at[:, first + rows - 1], abuf.at[:, 0], halo_send.at[to], halo_recv.at[0],
+            (img, 2 * (z + 1) + to),
+        )
+
+    def halo_down(to):
+        return remote(
+            abuf.at[:, first], abuf.at[:, span - 1], halo_send.at[to], halo_recv.at[1],
+            (img, 2 * (z - 1) + to),
+        )
+
+    sends_up = (core == 1) & (z < depth - 1)
+    sends_down = (core == 0) & (z > 0)
+
+    @pl.when(sends_up)
+    def _():
+        halo_up(0).start()
+        halo_up(1).start()
+
+    @pl.when(sends_down)
+    def _():
+        halo_down(0).start()
+        halo_down(1).start()
+
+    def par_copy(step):
+        to = lax.rem(z + step, depth)
+        return remote(par_ref, pbuf.at[z], par_send.at[step], par_recv.at[z], (img, 2 * to + core))
+
+    for step in range(1, depth):
+        par_copy(step).start()
+    pbuf[z] = par_ref[...]
 
     def forward_z(p):
         for dist in range(1, depth):
@@ -230,13 +247,32 @@
             arrived(zz, p, img_x)
             arrived(zz, p, img_y)
 
-            @pl.when(zz % 2 == 0)
+            @pl.when((zz % 2 == z % 2) & (zz < depth // 2))
             def _():
                 w_copy(1, wbuf.at[zz, p, img_x], zz, p, img_x).start()
 
-            @pl.when(zz % 2 == 1)
+            @pl.when((zz % 2 == z % 2) & (zz >= depth // 2))
             def _():
                 w_copy(0, wbuf.at[zz, p, img_y], zz, p, img_y).start()
+
+    def forward_diagonal(p):
+        for zz in range(depth):
+            @pl.when(zz % 2 == z % 2)
+            def _():
+                arrived(zz, p, img_d)
+
+                @pl.when(z % 2 == 0)
+                def _():
+                    w_copy(2, wbuf.at[zz, p, img_d], zz, p, img_d).start()
+
+                @pl.when(z % 2 == 1)
+                def _():
+                    w_copy(3, wbuf.at[zz, p, img_d], zz, p, img_d).start()
+
+    def take_diagonal(zz, p):
+        @pl.when(zz % 2 != z % 2)
+        def _():
+            arrived(zz, p, img_d)
 
     def out_copy(step):
         p, q = step // 2, step % 2
@@ -245,6 +281,9 @@
         )
 
     row_id = lax.broadcasted_iota(jnp.int32, (cols, 128), 0)
+
+    def params(zz, p):
+        return pbuf[zz, :, pl.ds(pl.multiple_of(p * PIECE, PIECE), PIECE)].astype(jnp.float32)
 
     def compute(step):
         p, q = step // 2, step % 2
@@ -259,7 +298,7 @@
                 return 0
 
             lax.fori_loop(0, 2, product, 0)
-            bias = pbuf[zz, p][0:1].astype(jnp.float32)
+            bias = params(zz, p)[0:1]
 
             def activation(r, _):
                 value, slope = act_slope(ebuf[half, 0, r] + bias)
@@ -271,7 +310,7 @@
 
             lax.fori_loop(0, span, activation, 0)
 
-        par = [pbuf[q, p].astype(jnp.float32), pbuf[q + depth // 2, p].astype(jnp.float32)]
+        par = [params(q, p), params(q + depth // 2, p)]
 
         def mixed(half, t, o, lanes):
             taps = par[half][:, lanes]
@@ -318,13 +357,7 @@
         lax.fori_loop(0, rows, ours, 0)
 
     for p in range(pieces):
-        own_sends(p)
-
-    def place(p, _):
-        wbuf[z, p, img] = w_ref[p]
-        return 0
-
-    lax.fori_loop(0, pieces, place, 0)
+        wbuf[z, p, img] = w_ref[:, p * PIECE : (p + 1) * PIECE]
 
     @pl.when(z == 0)
     def _():
@@ -338,7 +371,6 @@
     forward_xy(0)
     lax.fori_loop(2, pieces, lambda p, _: (forward_z(p), 0)[1], 0)
 
-    keep.wait()
     share.wait()
 
     @pl.when(z > 0)
@@ -362,8 +394,12 @@
         def _():
             forward_xy(p + 1)
 
-        arrived(q, p, img_d)
-        arrived(q + depth // 2, p, img_d)
+        @pl.when(q == 0)
+        def _():
+            forward_diagonal(p)
+
+        take_diagonal(q, p)
+        take_diagonal(q + depth // 2, p)
         compute(step)
         return 0
 
@@ -384,20 +420,31 @@
 
     def sent(p, _):
         for zz in range(depth):
-            w_copy(0, w_ref.at[p], zz, p, img).wait_send()
-            w_copy(1, w_ref.at[p], zz, p, img).wait_send()
-            if zz % 2 == 0:
-                w_copy(1, w_ref.at[p], zz, p, img_x).wait_send()
-            else:
-                w_copy(0, w_ref.at[p], zz, p, img_y).wait_send()
+            w_copy(0, piece_of(p), zz, p, img).wait_send()
+            w_copy(1, piece_of(p), zz, p, img).wait_send()
+
+            @pl.when(zz % 2 == z % 2)
+            def _():
+                if zz < depth // 2:
+                    w_copy(1, piece_of(p), zz, p, img_x).wait_send()
+                else:
+                    w_copy(0, piece_of(p), zz, p, img_y).wait_send()
+
+                @pl.when(z % 2 == 0)
+                def _():
+                    w_copy(2, piece_of(p), zz, p, img_d).wait_send()
+
+                @pl.when(z % 2 == 1)
+                def _():
+                    w_copy(3, piece_of(p), zz, p, img_d).wait_send()
 
             @pl.when((z >= zz) & (z < depth - 1))
             def _():
-                w_copy(2, w_ref.at[p], zz, p, img).wait_send()
+                w_copy(2, piece_of(p), zz, p, img).wait_send()
 
             @pl.when((z <= zz) & (z > 0))
             def _():
-                w_copy(3, w_ref.at[p], zz, p, img).wait_send()
+                w_copy(3, piece_of(p), zz, p, img).wait_send()
 
         return 0
 
@@ -408,6 +455,25 @@
         return 0
 
     lax.fori_loop(0, 2 * pieces, returned, 0)
+
+    tiles = gated_ref.shape[3] // 128 // 2
+    met = tiles // 2
+
+    def finished(j, _):
+        for which, ref in enumerate((gated_ref, tangent_ref)):
+            for q in range(depth // 2):
+                for tile in range(tiles):
+                    blocks = []
+                    for side, index in ((0, tile), (1, tile - met)):
+                        if 0 <= index <= met:
+                            lanes = slice(index * 128 % PIECE, index * 128 % PIECE + 128)
+                            blocks.append(out_ref[2 * q + side, index * 128 // PIECE, which, j, :, lanes])
+                    block = blocks[0] if len(blocks) == 1 else blocks[0] + blocks[1]
+                    lane = (q * tiles + tile) * 128
+                    ref[0, j, :, lane : lane + 128] = block
+        return 0
+
+    lax.fori_loop(0, rows, finished, 0)
 
 
 def fused(latents, tangents, w_expand, b_expand, w_depth, b_depth):
@@ -417,27 +483,27 @@
     tall = round_up(part, 16)
     pieces = round_up(width, PIECE) // PIECE
     wide = pieces * PIECE
-    acts = jnp.stack([latents[0], tangents[0]]).reshape(2, rows, cols, parts, part)
-    acts = jnp.pad(acts, ((0, 0),) * 4 + ((0, tall - part),)).reshape(2, rows, cols, parts * tall)
-    weights = jnp.pad(w_expand, ((0, tall - part), (0, wide - width)))
-    weights = weights.reshape(tall, pieces, PIECE).transpose(1, 0, 2)
+    gap = (wide - width) * (lax.axis_index("band") % 2)
+    weights = lax.dynamic_update_slice(jnp.zeros((tall, wide), w_expand.dtype), w_expand, (0, gap))
     par = jnp.concatenate([b_expand[None], w_depth, b_depth[None]], 0)
-    par = jnp.pad(par, ((0, 16 - par.shape[0]), (0, wide - width)))
-    par = par.reshape(16, pieces, PIECE).transpose(1, 0, 2)
+    par = lax.dynamic_update_slice(jnp.zeros((16, wide), par.dtype), par, (0, gap))
     bf, f32 = jnp.bfloat16, jnp.float32
     dma = pltpu.SemaphoreType.DMA
-    out = pl.pallas_call(
+    result = jax.ShapeDtypeStruct((1, rows, cols, 4 * width), bf)
+    return pl.pallas_call(
         fused_kernel,
-        out_shape=jax.ShapeDtypeStruct((4, pieces, 2, rows, cols, PIECE), bf),
-        in_specs=[pl.BlockSpec(memory_space=pltpu.VMEM)] * 3,
-        out_specs=pl.BlockSpec(memory_space=pltpu.VMEM),
+        out_shape=(result, result),
+        in_specs=[pl.BlockSpec(memory_space=pltpu.VMEM)] * 4,
+        out_specs=[pl.BlockSpec(memory_space=pltpu.VMEM)] * 2,
         scratch_shapes=[
             pltpu.VMEM((2, 2 * rows + 2, cols, parts * tall), bf),
             pltpu.VMEM((4, pieces, parts, tall, PIECE), bf),
-            pltpu.VMEM((4, pieces, 16, PIECE), bf),
+            pltpu.VMEM((4, 16, wide), bf),
             pltpu.VMEM((2, 2, 2 * rows + 2, cols, PIECE), f32),
             pltpu.VMEM((2 * pieces, 2, rows, cols, PIECE), bf),
-            dma((3,)),
+            pltpu.VMEM((4, pieces, 2, rows, cols, PIECE), bf),
+            pltpu.VMEM((cols, parts * tall), f32),
+            dma((2,)),
             dma((2,)),
             dma((2,)),
             dma((4,)),
@@ -450,10 +516,7 @@
         compiler_params=pltpu.CompilerParams(
             collective_id=0, has_side_effects=True, vmem_limit_bytes=40 * 1024 * 1024
         ),
-    )(acts, weights, par)
-    out = out.transpose(2, 3, 4, 0, 1, 5).reshape(2, rows, cols, 4, wide)[..., :width]
-    out = out.reshape(2, 1, rows, cols, 4 * width)
-    return out[0], out[1]
+    )(latents, tangents, weights, par)
 
 
 def solution(mesh):

time: 103 us -> 95.7 us (0.929)
  local copies, waits for them, and re-layouts: 14 us -> 7.66 us
    dynamic_update_slice x0 -> x2, local copies, waits for them, and re-layouts: none -> 4.46 us  [the longest x1 3.89 us: fused(): lax.dynamic_update_slice(jnp.zeros((tall, wide), w_expand.dtype), w_expan...]
    reshape x5 -> x0, local copies, waits for them, and re-layouts: 4.13 us -> none  [the longest x1 2.9 us: fused(): out.transpose(2, 3, 4, 0, 1, 5).reshape(2, rows, cols, 4, wide)[..., :width]]
    squeeze x2 -> x0, local copies, waits for them, and re-layouts: 2.98 us -> none  [fused(): return (out[0], out[1])]
    slice x3 -> x0, local copies, waits for them, and re-layouts: 2.69 us -> none  [fused(): return (out[0], out[1])]
    unnamed x4 -> x10, local copies, waits for them, and re-layouts: 0.01 us -> 1.74 us
    pad x2 -> x0, local copies, waits for them, and re-layouts: 1.39 us -> none  [the longest x1 1.05 us: fused(): weights = jnp.pad(w_expand, ((0, tall - part), (0, wide - width)))]
    transpose x1 -> x0, local copies, waits for them, and re-layouts: 1.36 us -> none  [fused(): out.transpose(2, 3, 4, 0, 1, 5).reshape(2, rows, cols, 4, wide)[..., :width]]
where the time goes in v2:
time: 95.7 us; the launch traced here: 95.3 us
  Pallas kernels  86.9 us (91%)
  local copies, waits for them, and re-layouts  7.66 us (8%)
    pallas_call x1, Pallas kernels, fused(): pl.pallas_call(fused_kernel, out_shape=(result, result), in_specs=[pl.Blo...  86.9 us
    dynamic_update_slice x1, local copies, waits for them, and re-layouts, fused(): lax.dynamic_update_slice(jnp.zeros((tall, wide), w_expand.dtype), w_expan...  3.89 us

profile of v2, /device:TPU:0, one launch (start us, length us, event | category | flops | bytes accessed | tf_op | source)
XLA Modules:
  0.0 95.3 jit_solution(1656807856702021150)
XLA Ops:
  0.6 0.0 copy-start.3
  0.6 0.0 copy-start.2
  0.7 0.7 broadcast_in_dim.14
  1.4 0.7 broadcast_in_dim.15
  2.1 0.0 copy-done.3
  2.1 0.6 dynamic_update_slice.7.par_ref
  2.7 0.0 copy-done.2
  2.7 0.0 copy-start
  2.8 0.0 copy-start.1
  2.8 3.9 %dynamic_update_slice.6.w_ref = bf16[288,768]{1,0:T(8,128)(2,1)S(1)} dynamic-update-slice(bf16[288,768]{1,0:T(8,128)(2,1)S(1)} %broadcast_in_dim.12, bf16[280,704]{1,0:T(8,128)(2,1)S(1)} %copy-done.2, s32[]{:T(128)} %constant.9.clone.1, s32[]{:T(128)S(6)} %select_n.12) | dynamic-update-slice | bytes 788484 | tf_op jit(solution)/shard_map/dynamic_update_slice | solution.py:487
  6.7 0.0 copy-done
  6.7 0.0 copy-done.1
  6.7 86.9 %shard_map.77 = (bf16[1,2,64,2816]{3,2,1,0:T(8,128)(2,1)S(1)}, bf16[1,2,64,2816]{3,2,1,0:T(8,128)(2,1)S(1)}) custom-call(bf16[1,2,64,1120]{3,2,1,0:T(8,128)(2,1)S(1)} %copy-done, bf16[1,2,64,1120]{3,2,1,0:T(8,128)(2,1)S(1)} %copy-done.1, bf16[288,768]{1,0:T(8,128)(2,1)S(1)} %dynamic_update_slice.6.w_ref, bf16[16,768]{1,0:T(8,128)(2,1)S(1)} %dynamic_update_slice.7.par_ref), custom_call_target="tpu_custom_call" | custom-call | tf_op jit(solution)/shard_map/pallas_call | solution.py:493
  93.6 0.9 copy.12
  94.5 0.9 copy.13
  (3 shorter events, 0.1 us)
Async XLA Ops:
  0.6 1.5 %copy-start.3 = (bf16[9,704]{1,0:T(8,128)(2,1)S(1)}, bf16[9,704]{1,0:T(8,128)(2,1)}, u32[]{:S(2)}) copy-start(bf16[9,704]{1,0:T(8,128)(2,1)} %param.10) | copy-start | bytes 38020
  0.6 2.1 %copy-start.2 = (bf16[280,704]{1,0:T(8,128)(2,1)S(1)}, bf16[280,704]{1,0:T(8,128)(2,1)}, u32[]{:S(2)}) copy-start(bf16[280,704]{1,0:T(8,128)(2,1)} %param.8) | copy-start | bytes 1182724
  2.7 3.9 %copy-start = (bf16[1,2,64,1120]{3,2,1,0:T(8,128)(2,1)S(1)}, bf16[1,2,64,1120]{3,2,1,0:T(8,128)(2,1)}, u32[]{:S(2)}) copy-start(bf16[1,2,64,1120]{3,2,1,0:T(8,128)(2,1)} %latents_ref.1) | copy-start | bytes 860164
  2.8 3.9 %copy-start.1 = (bf16[1,2,64,1120]{3,2,1,0:T(8,128)(2,1)S(1)}, bf16[1,2,64,1120]{3,2,1,0:T(8,128)(2,1)}, u32[]{:S(2)}) copy-start(bf16[1,2,64,1120]{3,2,1,0:T(8,128)(2,1)} %tangents_ref.1) | copy-start | bytes 860164
